TPU v7x, 32 devices: a whole 2x2x4 slice. The times are simulated.
32 devices in a mesh: replica: 4 (over y, core), tensor: 8 (over z, x).
Axes of the slice: x: 2, y: 2, z: 4, core: 2. Of those that a mesh axis runs over, the one named last changes fastest.
Arguments:
- tokens: bfloat16 [4, 2048, 8192], P('replica', None, 'tensor'), may hold values from -6 to 6
- kv_grad: bfloat16 [4, 2048, 1024], P('replica', None, 'tensor'), may hold values from -6 to 6
- weights: float32 [4, 8192, 1024], P('replica', 'tensor'), may hold values from -0.0625 to 0.0625
- first_moment: bfloat16 [4, 8192, 1024], P('replica', 'tensor'), may hold values from -240 to 240
- second_moment: bfloat16 [4, 8192, 1024], P('replica', 'tensor'), may hold values from 300 to 5984
- exponent: int32 [8], replicated, may hold values from 0 to 1, as said below
Outputs:
- new_weights: float32 [4, 8192, 1024], P('replica', 'tensor')
- new_first: bfloat16 [4, 8192, 1024], P('replica', 'tensor')
- new_second: bfloat16 [4, 8192, 1024], P('replica', 'tensor')
- input_grad: bfloat16 [4, 2048, 8192], P('replica', None, 'tensor')
Inputs may be any that keep to these rules, and one draw needn't show every extreme that they name: One integer per column bucket; the gossip partner of bucket g lies 2 ** exponent[g] replicas away; some bucket takes 0 and some bucket takes the largest allowed value.
All inputs are finite; a program needn't handle non-finite values.
Results may differ from a plain program's by a relative error of at most 0.0049.
Values may be sent and summed in bfloat16 or wider, within the bound.
A program may use at most 128 MiB of HBM per device.

v0:
```python
import jax
import jax.numpy as jnp
from jax import lax
from jax.sharding import PartitionSpec as P

learn_rate = 0.00015
beta_first = 0.9
beta_second = 0.95
decay_rate = 0.1
epsilon = 1e-08


def for_sending(array):
    return jax.tree.map(lambda a: a.astype(jnp.bfloat16) if a.dtype == jnp.float32 else a, array)


def from_behind(array, axis, by):
    count = lax.axis_size(axis)
    return lax.ppermute(array, axis, [(i, (i + by) % count) for i in range(count)])


def build_branch(hop_count):

    def fetch_peer(source_array):
        return jax.tree.map(
            lambda part, own: part.astype(own.dtype),
            from_behind(for_sending(source_array), "replica", hop_count),
            source_array,
        )

    return fetch_peer


def bucket_gossip(source_array, exponent, builder):
    levels = lax.axis_size("replica").bit_length() - 1
    branches = [builder(1 << bit_index) for bit_index in range(levels)]
    bucket_count = exponent.shape[0]
    bucket_width = source_array.shape[2] // bucket_count
    pieces = []
    for bucket_index in range(bucket_count):
        columns = source_array[
            :, :, bucket_index * bucket_width : (bucket_index + 1) * bucket_width
        ]
        pieces.append(lax.switch(exponent[bucket_index], branches, columns))
    return jnp.concatenate(pieces, axis=2)


def adam_update(master_part, partner_part, grad_part, first_part, second_part):
    averaged = 0.5 * (master_part + partner_part)
    first = beta_first * first_part.astype(jnp.float32) + (1.0 - beta_first) * grad_part
    second = (
        beta_second * second_part.astype(jnp.float32) + (1.0 - beta_second) * grad_part * grad_part
    )
    direction = first / (jnp.sqrt(second) + epsilon)
    new_weights = averaged - learn_rate * (direction + decay_rate * averaged)
    return (new_weights, first.astype(jnp.bfloat16), second.astype(jnp.bfloat16))


def on_device(tokens, kv_grad, weights, first_moment, second_moment, exponent):
    acts = tokens[0]
    local_cols = kv_grad[0]
    master = weights[0]
    master_low = master.astype(jnp.bfloat16)
    whole_grad = lax.all_gather(local_cols, "tensor", axis=1, tiled=True)
    grad_here = jnp.dot(acts.T, whole_grad, preferred_element_type=jnp.float32)
    back = jnp.dot(whole_grad, master_low.T, preferred_element_type=jnp.float32)
    partner = bucket_gossip(weights, exponent, build_branch)
    new_weights, new_first, new_second = adam_update(
        master, partner[0], grad_here, first_moment[0], second_moment[0]
    )
    return (new_weights[None], new_first[None], new_second[None], back.astype(jnp.bfloat16)[None])


def solution(mesh):
    placed = (
        P("replica", None, "tensor"),
        P("replica", None, "tensor"),
        P("replica", "tensor", None),
        P("replica", "tensor", None),
        P("replica", "tensor", None),
        P(),
    )
    return jax.shard_map(
        on_device,
        mesh=mesh,
        in_specs=placed,
        out_specs=(
            P("replica", "tensor", None),
            P("replica", "tensor", None),
            P("replica", "tensor", None),
            P("replica", None, "tensor"),
        ),
        check_vma=False,
    )
```

profile of v0, /device:TPU:0, one launch (start us, length us, event | category | flops | bytes accessed | tf_op | source)
XLA Modules:
  0.0 116.2 jit_solution(7453863151235359083)
XLA Ops:
  7.9 1.6 %fusion.18 = (s32[1]{0:T(128)}, s32[1]{0:T(128)}, s32[1]{0:T(128)}, s32[1]{0:T(128)}, s32[1]{0:T(128)}, /*index=5*/s32[1]{0:T(128)}, s32[1]{0:T(128)}, s32[1]{0:T(128)}) fusion(s32[8]{0:T(128)} %param.27), kind=kLoop, calls=%fused_computation.28 | loop fusion | bytes 64 | tf_op jit(solution)/shard_map/slice | solution.py:44
  14.8 3.2 %fusion.17 = (bf16[1,1024,128]{2,1,0:T(8,128)(2,1)S(1)}, bf16[1,1024,128]{2,1,0:T(8,128)(2,1)}, bf16[1,1024,128]{2,1,0:T(8,128)(2,1)S(1)}, bf16[1,1024,128]{2,1,...) fusion(f32[1,1024,1024]{2,1,0:T(8,128)} %param.24), kind=kLoop, calls=%fused_computation.27 | loop fusion | bytes 4194304 | tf_op jit(solution)/shard_map/slice | solution.py:41
  18.0 6.5 %conditional.32 = (f32[1,1024,128]{2,1,0:T(8,128)S(1)}) conditional(s32[]{:T(128)} %bitcast, bf16[1,1024,128]{2,1,0:T(8,128)(2,1)S(1)} %get-tuple-element.102, bf16[1,1024,128]{2,1,0:T(8,128)(2,1)S(1)} %get-tuple-element.102), branch_computations={%region_0.0_spmd, %region_1.0_spmd} | conditional | flops 131072 | bytes 1835056
  18.5 6.0 %collective-permute-done = bf16[1,1024,128]{2,1,0:T(8,128)(2,1)S(1)} collective-permute-done((bf16[1,1024,128]{2,1,0:T(8,128)(2,1)S(1)}, bf16[1,1024,128]{2,1,0:T(8,128)(2,1)S(1)}, u32[]{:S(2)}, u32[]{:S(2)}) %collective-permute-start) | collective-permute-done | bytes 262176 | tf_op jit(solution)/shard_map/cond/branch_0_fun/ppermute | solution.py:19
  24.5 8.3 %conditional.33 = (f32[1,1024,128]{2,1,0:T(8,128)S(1)}) conditional(s32[]{:T(128)} %bitcast.1, bf16[1,1024,128]{2,1,0:T(8,128)(2,1)S(1)} %get-tuple-element.101, bf16[1,1024,128]{2,1,0:T(8,128)(2,1)S(1)} %get-tuple-element.101), branch_computations={%region_2.0_spmd, %region_3.0_spmd} | conditional | flops 131072 | bytes 1835056
  24.6 2.4 %collective-permute-start.3 = (bf16[1,1024,128]{2,1,0:T(8,128)(2,1)S(1)}, bf16[1,1024,128]{2,1,0:T(8,128)(2,1)S(1)}, u32[]{:S(2)}, u32[]{:S(2)}) collective-permute-start(bf16[1,1024,128]{2,1,0:T(8,128)(2,1)S(1)} %param.3), channel_id=1, source_target_pairs={{0,16},{8,24},{16,0},{24,8},{1,17},{9,25},{17,1},{25,9},{2,18},{10... | collective-permute-start | bytes 786440 | tf_op jit(solution)/shard_map/cond/branch_1_fun/ppermute | solution.py:19
  26.9 5.8 %collective-permute-done.3 = bf16[1,1024,128]{2,1,0:T(8,128)(2,1)S(1)} collective-permute-done((bf16[1,1024,128]{2,1,0:T(8,128)(2,1)S(1)}, bf16[1,1024,128]{2,1,0:T(8,128)(2,1)S(1)}, u32[]{:S(2)}, u32[]{:S(2)}) %collective-permute-start.3) | collective-permute-done | bytes 262176 | tf_op jit(solution)/shard_map/cond/branch_1_fun/ppermute | solution.py:19
  32.8 5.9 %conditional.34 = (f32[1,1024,128]{2,1,0:T(8,128)S(1)}) conditional(s32[]{:T(128)} %bitcast.2, bf16[1,1024,128]{2,1,0:T(8,128)(2,1)S(1)} %get-tuple-element.100, bf16[1,1024,128]{2,1,0:T(8,128)(2,1)S(1)} %get-tuple-element.100), branch_computations={%region_4.0_spmd, %region_5.0_spmd} | conditional | flops 131072 | bytes 1835056
  32.9 5.8 %collective-permute-done.4 = bf16[1,1024,128]{2,1,0:T(8,128)(2,1)S(1)} collective-permute-done((bf16[1,1024,128]{2,1,0:T(8,128)(2,1)S(1)}, bf16[1,1024,128]{2,1,0:T(8,128)(2,1)S(1)}, u32[]{:S(2)}, u32[]{:S(2)}) %collective-permute-start.4) | collective-permute-done | bytes 262176 | tf_op jit(solution)/shard_map/cond/branch_0_fun/ppermute | solution.py:19
  38.7 6.5 %conditional.35 = (f32[1,1024,128]{2,1,0:T(8,128)S(1)}) conditional(s32[]{:T(128)} %bitcast.3, bf16[1,1024,128]{2,1,0:T(8,128)(2,1)S(1)} %get-tuple-element.99, bf16[1,1024,128]{2,1,0:T(8,128)(2,1)S(1)} %get-tuple-element.99), branch_computations={%region_6.0_spmd, %region_7.0_spmd} | conditional | flops 131072 | bytes 1835056
  39.4 5.8 %collective-permute-done.7 = bf16[1,1024,128]{2,1,0:T(8,128)(2,1)S(1)} collective-permute-done((bf16[1,1024,128]{2,1,0:T(8,128)(2,1)S(1)}, bf16[1,1024,128]{2,1,0:T(8,128)(2,1)S(1)}, u32[]{:S(2)}, u32[]{:S(2)}) %collective-permute-start.7) | collective-permute-done | bytes 262176 | tf_op jit(solution)/shard_map/cond/branch_1_fun/ppermute | solution.py:19
  45.2 5.9 %conditional.36 = (f32[1,1024,128]{2,1,0:T(8,128)S(1)}) conditional(s32[]{:T(128)} %bitcast.4, bf16[1,1024,128]{2,1,0:T(8,128)(2,1)S(1)} %get-tuple-element.98, bf16[1,1024,128]{2,1,0:T(8,128)(2,1)S(1)} %get-tuple-element.98), branch_computations={%region_8.0_spmd, %region_9.0_spmd} | conditional | flops 131072 | bytes 1835056
  45.3 5.8 %collective-permute-done.8 = bf16[1,1024,128]{2,1,0:T(8,128)(2,1)S(1)} collective-permute-done((bf16[1,1024,128]{2,1,0:T(8,128)(2,1)S(1)}, bf16[1,1024,128]{2,1,0:T(8,128)(2,1)S(1)}, u32[]{:S(2)}, u32[]{:S(2)}) %collective-permute-start.8) | collective-permute-done | bytes 262176 | tf_op jit(solution)/shard_map/cond/branch_0_fun/ppermute | solution.py:19
  51.2 7.5 %conditional.37 = (f32[1,1024,128]{2,1,0:T(8,128)S(1)}) conditional(s32[]{:T(128)} %bitcast.5, bf16[1,1024,128]{2,1,0:T(8,128)(2,1)S(1)} %get-tuple-element.97, bf16[1,1024,128]{2,1,0:T(8,128)(2,1)S(1)} %get-tuple-element.97), branch_computations={%region_10.0_spmd, %region_11.0_spmd} | conditional | flops 131072 | bytes 1835056
  51.2 1.6 %collective-permute-start.11 = (bf16[1,1024,128]{2,1,0:T(8,128)(2,1)S(1)}, bf16[1,1024,128]{2,1,0:T(8,128)(2,1)S(1)}, u32[]{:S(2)}, u32[]{:S(2)}) collective-permute-start(bf16[1,1024,128]{2,1,0:T(8,128)(2,1)S(1)} %param.11), channel_id=1, source_target_pairs={{0,16},{8,24},{16,0},{24,8},{1,17},{9,25},{17,1},{25,9},{2,18},{10... | collective-permute-start | bytes 786440 | tf_op jit(solution)/shard_map/cond/branch_1_fun/ppermute | solution.py:19
  52.7 5.8 %collective-permute-done.11 = bf16[1,1024,128]{2,1,0:T(8,128)(2,1)S(1)} collective-permute-done((bf16[1,1024,128]{2,1,0:T(8,128)(2,1)S(1)}, bf16[1,1024,128]{2,1,0:T(8,128)(2,1)S(1)}, u32[]{:S(2)}, u32[]{:S(2)}) %collective-permute-start.11) | collective-permute-done | bytes 262176 | tf_op jit(solution)/shard_map/cond/branch_1_fun/ppermute | solution.py:19
  58.6 7.7 %conditional.38 = (f32[1,1024,128]{2,1,0:T(8,128)}) conditional(s32[]{:T(128)} %bitcast.6, bf16[1,1024,128]{2,1,0:T(8,128)(2,1)} %get-tuple-element.96, bf16[1,1024,128]{2,1,0:T(8,128)(2,1)} %get-tuple-element.96), branch_computations={%region_12.0_spmd, %region_13.0_spmd} | conditional | flops 131072 | bytes 1835056
  59.2 6.2 %collective-permute-done.13 = bf16[1,1024,128]{2,1,0:T(8,128)(2,1)S(1)} collective-permute-done((bf16[1,1024,128]{2,1,0:T(8,128)(2,1)}, bf16[1,1024,128]{2,1,0:T(8,128)(2,1)S(1)}, u32[]{:S(2)}, u32[]{:S(2)}) %collective-permute-start.13) | collective-permute-done | bytes 262176 | tf_op jit(solution)/shard_map/cond/branch_1_fun/ppermute | solution.py:19
  65.5 0.8 convert_element_type.155
  66.3 6.6 %conditional.39 = (f32[1,1024,128]{2,1,0:T(8,128)}) conditional(s32[]{:T(128)} %bitcast.7, bf16[1,1024,128]{2,1,0:T(8,128)(2,1)S(1)} %get-tuple-element.95, bf16[1,1024,128]{2,1,0:T(8,128)(2,1)S(1)} %get-tuple-element.95), branch_computations={%region_14.0_spmd, %region_15.0_spmd} | conditional | flops 131072 | bytes 1835056
  66.3 5.8 %collective-permute-done.14 = bf16[1,1024,128]{2,1,0:T(8,128)(2,1)S(1)} collective-permute-done((bf16[1,1024,128]{2,1,0:T(8,128)(2,1)S(1)}, bf16[1,1024,128]{2,1,0:T(8,128)(2,1)S(1)}, u32[]{:S(2)}, u32[]{:S(2)}) %collective-permute-start.14) | collective-permute-done | bytes 262176 | tf_op jit(solution)/shard_map/cond/branch_0_fun/ppermute | solution.py:19
  72.1 0.8 convert_element_type.157
  72.9 0.8 constant_dynamic-update-slice_fusion.7
  73.7 0.8 constant_dynamic-update-slice_fusion.6
  74.6 0.8 constant_dynamic-update-slice_fusion.5
  75.4 0.8 constant_dynamic-update-slice_fusion.4
  76.2 0.8 constant_dynamic-update-slice_fusion.3
  77.9 0.8 constant_dynamic-update-slice_fusion.1
  78.7 0.8 constant_dynamic-update-slice_fusion
  79.5 8.2 %all-gather.3.cloned.1.call-done = bf16[1,2048,1024]{2,1,0:T(8,128)(2,1)} async-done(((bf16[1,2048,128]{2,1,0:T(8,128)(2,1)}), bf16[1,2048,1024]{2,1,0:T(8,128)(2,1)}) %all-gather.3.cloned.1.call-update) | async-done | bytes 4194320 | tf_op jit(solution)/shard_map/all_gather | solution.py:64
  87.8 10.2 %convert_bitcast_fusion = bf16[1,2048,1024]{2,1,0:T(8,128)(2,1)} fusion(bf16[1,2048,1024]{2,1,0:T(8,128)(2,1)} %all-gather.3.cloned.1.call-done, f32[1,1024,1024]{2,1,0:T(8,128)} %param.24), kind=kOutput, calls=%fused_computation.12 | convolution fusion | flops 4298113024 | bytes 12582912 | tf_op jit(solution)/shard_map/dot_general | solution.py:66
  98.0 11.3 %fusion.13 = (bf16[1,1024,1024]{2,1,0:T(8,128)(2,1)}, f32[1,1024,1024]{2,1,0:T(8,128)}, bf16[1,1024,1024]{2,1,0:T(8,128)(2,1)}) fusion(bf16[1,1024,1024]{2,1,0:T(8,128)(2,1)S(1)} %copy-done.5, bf16[1,1024,1024]{2,1,0:T(8,128)(2,1)S(1)} %copy-done.6, f32[1,1024,1024]{2,1,0:T(8,128)S(1)} %copy-done.2, f32[1,1024,1024]{2,1,0:T(8,128)} %constant_dynamic-update-slice_fusion, ...), kind=kOutput, calls=%fused_computation.15 | convolution fusion | flops 4314890240 | bytes 29360128 | tf_op jit(solution)/shard_map/dot_general | solution.py:65
  (29 shorter events, 3.5 us)
Async XLA Ops:
  7.2 80.6 %all-gather.3.cloned.1.call-start = ((), (), s32[]{:S(2)}) async-start(), calls=%async_computation | async-start | bytes 4718592 | tf_op jit(solution)/shard_map/all_gather | solution.py:64
  18.0 6.5 %collective-permute-start = (bf16[1,1024,128]{2,1,0:T(8,128)(2,1)S(1)}, bf16[1,1024,128]{2,1,0:T(8,128)(2,1)S(1)}, u32[]{:S(2)}, u32[]{:S(2)}) collective-permute-start(bf16[1,1024,128]{2,1,0:T(8,128)(2,1)S(1)} %param), channel_id=1, source_target_pairs={{0,8},{8,16},{16,24},{24,0},{1,9},{9,17},{17,25},{25,1},{2,10},{10... | collective-permute-start | bytes 786440 | tf_op jit(solution)/shard_map/cond/branch_0_fun/ppermute | solution.py:19
  24.6 8.2 %collective-permute-start.3 = (bf16[1,1024,128]{2,1,0:T(8,128)(2,1)S(1)}, bf16[1,1024,128]{2,1,0:T(8,128)(2,1)S(1)}, u32[]{:S(2)}, u32[]{:S(2)}) collective-permute-start(bf16[1,1024,128]{2,1,0:T(8,128)(2,1)S(1)} %param.3), channel_id=1, source_target_pairs={{0,16},{8,24},{16,0},{24,8},{1,17},{9,25},{17,1},{25,9},{2,18},{10... | collective-permute-start | bytes 786440 | tf_op jit(solution)/shard_map/cond/branch_1_fun/ppermute | solution.py:19
  32.8 5.8 %collective-permute-start.4 = (bf16[1,1024,128]{2,1,0:T(8,128)(2,1)S(1)}, bf16[1,1024,128]{2,1,0:T(8,128)(2,1)S(1)}, u32[]{:S(2)}, u32[]{:S(2)}) collective-permute-start(bf16[1,1024,128]{2,1,0:T(8,128)(2,1)S(1)} %param.4), channel_id=1, source_target_pairs={{0,8},{8,16},{16,24},{24,0},{1,9},{9,17},{17,25},{25,1},{2,10},{10... | collective-permute-start | bytes 786440 | tf_op jit(solution)/shard_map/cond/branch_0_fun/ppermute | solution.py:19
  38.8 6.4 %collective-permute-start.7 = (bf16[1,1024,128]{2,1,0:T(8,128)(2,1)S(1)}, bf16[1,1024,128]{2,1,0:T(8,128)(2,1)S(1)}, u32[]{:S(2)}, u32[]{:S(2)}) collective-permute-start(bf16[1,1024,128]{2,1,0:T(8,128)(2,1)S(1)} %param.7), channel_id=1, source_target_pairs={{0,16},{8,24},{16,0},{24,8},{1,17},{9,25},{17,1},{25,9},{2,18},{10... | collective-permute-start | bytes 786440 | tf_op jit(solution)/shard_map/cond/branch_1_fun/ppermute | solution.py:19
  45.3 5.8 %collective-permute-start.8 = (bf16[1,1024,128]{2,1,0:T(8,128)(2,1)S(1)}, bf16[1,1024,128]{2,1,0:T(8,128)(2,1)S(1)}, u32[]{:S(2)}, u32[]{:S(2)}) collective-permute-start(bf16[1,1024,128]{2,1,0:T(8,128)(2,1)S(1)} %param.8), channel_id=1, source_target_pairs={{0,8},{8,16},{16,24},{24,0},{1,9},{9,17},{17,25},{25,1},{2,10},{10... | collective-permute-start | bytes 786440 | tf_op jit(solution)/shard_map/cond/branch_0_fun/ppermute | solution.py:19
  51.2 7.4 %collective-permute-start.11 = (bf16[1,1024,128]{2,1,0:T(8,128)(2,1)S(1)}, bf16[1,1024,128]{2,1,0:T(8,128)(2,1)S(1)}, u32[]{:S(2)}, u32[]{:S(2)}) collective-permute-start(bf16[1,1024,128]{2,1,0:T(8,128)(2,1)S(1)} %param.11), channel_id=1, source_target_pairs={{0,16},{8,24},{16,0},{24,8},{1,17},{9,25},{17,1},{25,9},{2,18},{10... | collective-permute-start | bytes 786440 | tf_op jit(solution)/shard_map/cond/branch_1_fun/ppermute | solution.py:19
  58.6 6.8 %collective-permute-start.13 = (bf16[1,1024,128]{2,1,0:T(8,128)(2,1)}, bf16[1,1024,128]{2,1,0:T(8,128)(2,1)S(1)}, u32[]{:S(2)}, u32[]{:S(2)}) collective-permute-start(bf16[1,1024,128]{2,1,0:T(8,128)(2,1)} %param.13), channel_id=1, source_target_pairs={{0,16},{8,24},{16,0},{24,8},{1,17},{9,25},{17,1},{25,9},{2,18},{10... | collective-permute-start | bytes 786440 | tf_op jit(solution)/shard_map/cond/branch_1_fun/ppermute | solution.py:19
  66.3 5.8 %collective-permute-start.14 = (bf16[1,1024,128]{2,1,0:T(8,128)(2,1)S(1)}, bf16[1,1024,128]{2,1,0:T(8,128)(2,1)S(1)}, u32[]{:S(2)}, u32[]{:S(2)}) collective-permute-start(bf16[1,1024,128]{2,1,0:T(8,128)(2,1)S(1)} %param.14), channel_id=1, source_target_pairs={{0,8},{8,16},{16,24},{24,0},{1,9},{9,17},{17,25},{25,1},{2,10},{10... | collective-permute-start | bytes 786440 | tf_op jit(solution)/shard_map/cond/branch_0_fun/ppermute | solution.py:19
  72.9 5.0 %copy-start = (f32[1,1024,128]{2,1,0:T(8,128)S(1)}, f32[1,1024,128]{2,1,0:T(8,128)}, u32[]{:S(2)}) copy-start(f32[1,1024,128]{2,1,0:T(8,128)} %get-tuple-element.117) | copy-start | bytes 1572868
  72.9 5.8 %copy-start.1 = (f32[1,1024,128]{2,1,0:T(8,128)S(1)}, f32[1,1024,128]{2,1,0:T(8,128)}, u32[]{:S(2)}) copy-start(f32[1,1024,128]{2,1,0:T(8,128)} %get-tuple-element.118) | copy-start | bytes 1572868
  87.8 10.2 %copy-start.2 = (f32[1,1024,1024]{2,1,0:T(8,128)S(1)}, f32[1,1024,1024]{2,1,0:T(8,128)}, u32[]{:S(2)}) copy-start(f32[1,1024,1024]{2,1,0:T(8,128)} %param.24) | copy-start | bytes 12582916
  87.8 10.2 %copy-start.3 = (bf16[1,2048,1024]{2,1,0:T(8,128)(2,1)S(1)}, bf16[1,2048,1024]{2,1,0:T(8,128)(2,1)}, u32[]{:S(2)}) copy-start(bf16[1,2048,1024]{2,1,0:T(8,128)(2,1)} %param.22) | copy-start | bytes 12582916
  87.8 10.2 %copy-start.4 = (bf16[1,2048,1024]{2,1,0:T(8,128)(2,1)S(1)}, bf16[1,2048,1024]{2,1,0:T(8,128)(2,1)}, u32[]{:S(2)}) copy-start(bf16[1,2048,1024]{2,1,0:T(8,128)(2,1)} %all-gather.3.cloned.1.call-done) | copy-start | bytes 12582916
  87.8 10.2 %copy-start.5 = (bf16[1,1024,1024]{2,1,0:T(8,128)(2,1)S(1)}, bf16[1,1024,1024]{2,1,0:T(8,128)(2,1)}, u32[]{:S(2)}) copy-start(bf16[1,1024,1024]{2,1,0:T(8,128)(2,1)} %param.26) | copy-start | bytes 6291460
  87.8 10.2 %copy-start.6 = (bf16[1,1024,1024]{2,1,0:T(8,128)(2,1)S(1)}, bf16[1,1024,1024]{2,1,0:T(8,128)(2,1)}, u32[]{:S(2)}) copy-start(bf16[1,1024,1024]{2,1,0:T(8,128)(2,1)} %param.25) | copy-start | bytes 6291460
Sparse Core Ops, SparseCore 0:
  10.0 77.7 all-gather.2
where the time goes:
time: 116 us
  waiting for transfers between devices  56 us (48%)
  matrix products  21.5 us (19%)
  between operations  19.3 us (17%)
  local copies, waits for them, and re-layouts  11.5 us (10%)
  starting transfers between devices  5.73 us (5%)
  other arithmetic  1.87 us (2%)
    ppermute x8, waiting for transfers between devices, from_behind(): lax.ppermute(array, axis, [(i, (i + by) % count) for i in range(count)])  47.1 us
    dot_general x1, matrix products, on_device(): grad_here = jnp.dot(acts.T, whole_grad, preferred_element_type=jnp.float32)  11.3 us
    dot_general x1, matrix products, on_device(): back = jnp.dot(whole_grad, master_low.T, preferred_element_type=jnp.float32)  10.2 us
    all_gather x1, waiting for transfers between devices, on_device(): whole_grad = lax.all_gather(local_cols, 'tensor', axis=1, tiled=True)  8.25 us
    unnamed x21, local copies, waits for them, and re-layouts  5.81 us
    ppermute x8, starting transfers between devices, from_behind(): lax.ppermute(array, axis, [(i, (i + by) % count) for i in range(count)])  5.69 us
    slice x1, local copies, waits for them, and re-layouts, bucket_gossip(): source_array[:, :, bucket_index * bucket_width:(bucket_index + 1) * bucke...  3.25 us
  transfers between devices with their start and end apart: 9, of which 9 were waited for; matrix products, arithmetic and copies ran while one was open for 12% of the time, Pallas kernels for 0%

commit v1 on v0

--- a/solution.py
+++ b/solution.py
@@ -1,6 +1,8 @@
 import jax
 import jax.numpy as jnp
 from jax import lax
+from jax.experimental import pallas as pl
+from jax.experimental.pallas import tpu as pltpu
 from jax.sharding import PartitionSpec as P
 
 learn_rate = 0.00015
@@ -71,7 +73,297 @@
     return (new_weights[None], new_first[None], new_second[None], back.astype(jnp.bfloat16)[None])
 
 
+CHUNKS = 4
+PLANES = 4
+BLOCKS = 8
+TILE = 256
+
+
+def fused_kernel(
+    exponent, tokens, kv_grad, weights, first_moment, second_moment,
+    new_weights, new_first, new_second, input_grad,
+    gathered, tok, tok_t, master, low, other, outgoing, incoming, first_in, second_in, grad_acc, back_acc,
+    up_sem, down_sem, across_sem, block_sem, core_send, core_recv, peer_send, peer_recv,
+    own_sem, master_sem, tok_sem, first_sem, second_sem,
+):
+    replica = lax.axis_index("replica")
+    place = lax.axis_index("tensor")
+    core = lax.rem(replica, 2)
+    z = lax.div(place, 2)
+    x = lax.rem(place, 2)
+    rows_of = tokens.shape[0] // CHUNKS
+    width = kv_grad.shape[1]
+    depth = weights.shape[0]
+
+    above = {"tensor": lax.rem(place + 2, 2 * PLANES)}
+    below = {"tensor": lax.rem(place + 2 * PLANES - 2, 2 * PLANES)}
+    across = {"tensor": place + 1 - 2 * x}
+    twin = {"replica": replica + 1 - 2 * core}
+    peer = {"replica": lax.rem(replica + 2, 4)}
+    has_above = z < PLANES - 1
+    has_below = z > 0
+
+    order = [
+        z,
+        jnp.where(z == 0, 1, z - 1),
+        jnp.where(z == 0, 2, jnp.where(z == 1, 2, jnp.where(z == 2, 3, 1))),
+        jnp.where(z < 2, 3, 0),
+    ]
+
+    def rows(c):
+        return pl.ds(c * rows_of, rows_of)
+
+    def columns(g):
+        return pl.ds(pl.multiple_of(g * width, width), width)
+
+    def hop(plane, c, target, send_sem):
+        block = plane * 2 + x
+        piece = gathered.at[block, rows(c)]
+        return pltpu.make_async_remote_copy(
+            src_ref=piece, dst_ref=piece, send_sem=send_sem.at[plane, c], recv_sem=block_sem.at[block, c],
+            device_id=target, device_id_type=pl.DeviceIdType.MESH,
+        )
+
+    def arrived(block, c):
+        piece = gathered.at[block, rows(c)]
+        pltpu.make_async_remote_copy(
+            src_ref=piece, dst_ref=piece, send_sem=across_sem.at[0, 0], recv_sem=block_sem.at[block, c],
+            device_id=across, device_id_type=pl.DeviceIdType.MESH,
+        ).wait_recv()
+
+    def to_twin(g):
+        return pltpu.make_async_remote_copy(
+            src_ref=low.at[g], dst_ref=other.at[g], send_sem=core_send.at[g], recv_sem=core_recv.at[g],
+            device_id=twin, device_id_type=pl.DeviceIdType.MESH,
+        )
+
+    def to_peer(g):
+        return pltpu.make_async_remote_copy(
+            src_ref=outgoing.at[g], dst_ref=incoming.at[g], send_sem=peer_send.at[g], recv_sem=peer_recv.at[g],
+            device_id=peer, device_id_type=pl.DeviceIdType.MESH,
+        )
+
+    load_own = pltpu.make_async_copy(kv_grad, gathered.at[place], own_sem)
+    load_own.start()
+
+    def load_master(g):
+        return pltpu.make_async_copy(weights.at[:, columns(g)], master.at[:, columns(g)], master_sem.at[g])
+
+    buckets = [order[i // 2] * 2 + i % 2 for i in range(BLOCKS)]
+    for g in buckets:
+        load_master(g).start()
+    load_tok = [pltpu.make_async_copy(tokens.at[rows(c)], tok.at[rows(c)], tok_sem.at[c]) for c in range(CHUNKS)]
+    for copy in load_tok:
+        copy.start()
+    load_first = pltpu.make_async_copy(first_moment, first_in, first_sem)
+    load_second = pltpu.make_async_copy(second_moment, second_in, second_sem)
+    load_first.start()
+    load_second.start()
+
+    barrier = pltpu.get_barrier_semaphore()
+    for target in (across, twin, peer):
+        pl.semaphore_signal(barrier, inc=1, device_id=target, device_id_type=pl.DeviceIdType.MESH)
+
+    @pl.when(has_above)
+    def _():
+        pl.semaphore_signal(barrier, inc=1, device_id=above, device_id_type=pl.DeviceIdType.MESH)
+
+    @pl.when(has_below)
+    def _():
+        pl.semaphore_signal(barrier, inc=1, device_id=below, device_id_type=pl.DeviceIdType.MESH)
+
+    pl.semaphore_wait(barrier, 3 + has_above.astype(jnp.int32) + has_below.astype(jnp.int32))
+
+    load_own.wait()
+    for c in range(CHUNKS):
+        @pl.when(has_above)
+        def _():
+            hop(z, c, above, up_sem).start()
+
+        @pl.when(has_below)
+        def _():
+            hop(z, c, below, down_sem).start()
+
+        hop(z, c, across, across_sem).start()
+
+    for g in buckets:
+        load_master(g).wait()
+        low[g] = master[:, columns(g)].astype(jnp.bfloat16)
+        to_twin(g).start()
+
+        @pl.when(core == 1)
+        def _():
+            outgoing[g] = low[g]
+            to_peer(g).start()
+
+    for g in buckets:
+        to_twin(g).wait_recv()
+
+        @pl.when(core == 0)
+        def _():
+            near = jnp.full((16, width), exponent[g], jnp.int32).astype(jnp.float32)
+            near = jnp.where(near == 0.0, 1.0, 0.0)[0:1]
+            outgoing[g] = (
+                other[g].astype(jnp.float32) * near + low[g].astype(jnp.float32) * (1.0 - near)
+            ).astype(jnp.bfloat16)
+            to_peer(g).start()
+
+    for c in range(CHUNKS):
+        load_tok[c].wait()
+        tok_t[:, rows(c)] = tok[rows(c), :].T
+
+    def multiply(plane, c, last):
+        start = pl.multiple_of(c * rows_of, rows_of)
+        part = pl.ds(start, rows_of)
+
+        def piece():
+            return jnp.concatenate([gathered[plane * 2, part], gathered[plane * 2 + 1, part]], axis=1)
+
+        @pl.loop(0, depth // TILE)
+        def _(i):
+            tile = pl.ds(pl.multiple_of(i * TILE, TILE), TILE)
+            term = jnp.dot(tok_t[tile, part], piece(), preferred_element_type=jnp.float32)
+            grad_acc[tile, :] = jnp.where(c == 0, term, grad_acc[tile, :] + term) if not isinstance(c, int) else (
+                term if c == 0 else grad_acc[tile, :] + term
+            )
+
+        @pl.loop(0, depth // TILE)
+        def _(i):
+            tile = pl.ds(pl.multiple_of(i * TILE, TILE), TILE)
+            weight = jnp.concatenate([low[plane * 2, tile], low[plane * 2 + 1, tile]], axis=1)
+            term = lax.dot_general(piece(), weight, (((1,), (1,)), ((), ())), preferred_element_type=jnp.float32)
+            if last == "first":
+                back_acc[part, tile] = term
+            elif last == "middle":
+                back_acc[part, tile] += term
+            else:
+                input_grad[part, tile] = (back_acc[part, tile] + term).astype(jnp.bfloat16)
+
+    def update(plane):
+        for side in range(2):
+            g = plane * 2 + side
+            to_peer(g).wait_recv()
+            near = jnp.full((16, width), exponent[g], jnp.int32).astype(jnp.float32)
+            near = jnp.where(near == 0.0, 1.0, 0.0)[0:1] * core.astype(jnp.float32)
+
+            @pl.loop(0, depth // TILE)
+            def _(i):
+                tile = pl.ds(pl.multiple_of(i * TILE, TILE), TILE)
+                at = columns(g)
+                grad = grad_acc[tile, side * width:(side + 1) * width]
+                partner = (
+                    other[g, tile].astype(jnp.float32) * near
+                    + incoming[g, tile].astype(jnp.float32) * (1.0 - near)
+                )
+                averaged = 0.5 * (master[tile, at] + partner)
+                first = beta_first * first_in[tile, at].astype(jnp.float32) + (1.0 - beta_first) * grad
+                second = (
+                    beta_second * second_in[tile, at].astype(jnp.float32)
+                    + (1.0 - beta_second) * grad * grad
+                )
+                direction = first / (jnp.sqrt(second) + epsilon)
+                new_weights[tile, at] = averaged - learn_rate * (direction + decay_rate * averaged)
+                new_first[tile, at] = first.astype(jnp.bfloat16)
+                new_second[tile, at] = second.astype(jnp.bfloat16)
+
+    for phase in range(1, PLANES + 1):
+        for c in range(CHUNKS):
+            if phase < PLANES:
+                @pl.when(z - phase >= 0)
+                def _():
+                    plane = lax.rem(z - phase + PLANES, PLANES)
+                    arrived(plane * 2 + x, c)
+
+                    @pl.when(has_above)
+                    def _():
+                        hop(plane, c, above, up_sem).start()
+
+                @pl.when(z + phase < PLANES)
+                def _():
+                    plane = lax.rem(z + phase, PLANES)
+                    arrived(plane * 2 + x, c)
+
+                    @pl.when(has_below)
+                    def _():
+                        hop(plane, c, below, down_sem).start()
+
+                hop(order[phase], c, across, across_sem).start()
+            plane = order[phase - 1]
+            arrived(plane * 2 + 1 - x, c)
+            multiply(plane, c, "first" if phase == 1 else "middle" if phase < PLANES else "last")
+        if phase == 1:
+            load_first.wait()
+            load_second.wait()
+        update(plane)
+
+    for c in range(CHUNKS):
+        for plane in range(PLANES):
+            hop(plane, c, across, across_sem).wait_send()
+
+            @pl.when(jnp.logical_and(has_above, plane <= z))
+            def _():
+                hop(plane, c, above, up_sem).wait_send()
+
+            @pl.when(jnp.logical_and(has_below, plane >= z))
+            def _():
+                hop(plane, c, below, down_sem).wait_send()
+
+    for g in range(BLOCKS):
+        to_twin(g).wait_send()
+        to_peer(g).wait_send()
+
+
+def on_device_fused(tokens, kv_grad, weights, first_moment, second_moment, exponent):
+    tok, width, depth = tokens.shape[1], kv_grad.shape[2], weights.shape[1]
+    bf16, f32 = jnp.bfloat16, jnp.float32
+    wide = width * BLOCKS
+    any_space = pl.BlockSpec(memory_space=pl.ANY)
+    outs = pl.pallas_call(
+        fused_kernel,
+        out_shape=(
+            pltpu.VMEM((depth, wide), f32),
+            pltpu.VMEM((depth, wide), bf16),
+            pltpu.VMEM((depth, wide), bf16),
+            pltpu.VMEM((tok, depth), bf16),
+        ),
+        in_specs=[pl.BlockSpec(memory_space=pltpu.SMEM)] + [any_space] * 5,
+        out_specs=[pl.BlockSpec(memory_space=pltpu.VMEM)] * 4,
+        scratch_shapes=[
+            pltpu.VMEM((BLOCKS, tok, width), bf16),
+            pltpu.VMEM((tok, depth), bf16),
+            pltpu.VMEM((depth, tok), bf16),
+            pltpu.VMEM((depth, wide), f32),
+            pltpu.VMEM((BLOCKS, depth, width), bf16),
+            pltpu.VMEM((BLOCKS, depth, width), bf16),
+            pltpu.VMEM((BLOCKS, depth, width), bf16),
+            pltpu.VMEM((BLOCKS, depth, width), bf16),
+            pltpu.VMEM((depth, wide), bf16),
+            pltpu.VMEM((depth, wide), bf16),
+            pltpu.VMEM((depth, 2 * width), f32),
+            pltpu.VMEM((tok, depth), f32),
+            pltpu.SemaphoreType.DMA((PLANES, CHUNKS)),
+            pltpu.SemaphoreType.DMA((PLANES, CHUNKS)),
+            pltpu.SemaphoreType.DMA((PLANES, CHUNKS)),
+            pltpu.SemaphoreType.DMA((BLOCKS, CHUNKS)),
+            pltpu.SemaphoreType.DMA((BLOCKS,)),
+            pltpu.SemaphoreType.DMA((BLOCKS,)),
+            pltpu.SemaphoreType.DMA((BLOCKS,)),
+            pltpu.SemaphoreType.DMA((BLOCKS,)),
+            pltpu.SemaphoreType.DMA,
+            pltpu.SemaphoreType.DMA((BLOCKS,)),
+            pltpu.SemaphoreType.DMA((CHUNKS,)),
+            pltpu.SemaphoreType.DMA,
+            pltpu.SemaphoreType.DMA,
+        ],
+        compiler_params=pltpu.CompilerParams(
+            collective_id=0, has_side_effects=True, vmem_limit_bytes=46 << 20
+        ),
+    )(exponent, tokens[0], kv_grad[0], weights[0], first_moment[0], second_moment[0])
+    return tuple(out[None] for out in outs)
+
+
 def solution(mesh):
+    small = mesh.shape["replica"] == 4 and mesh.shape["tensor"] == BLOCKS
     placed = (
         P("replica", None, "tensor"),
         P("replica", None, "tensor"),
@@ -81,7 +373,7 @@
         P(),
     )
     return jax.shard_map(
-        on_device,
+        on_device_fused if small else on_device,
         mesh=mesh,
         in_specs=placed,
         out_specs=(

time: 116 us -> 64.4 us (0.56)
  Pallas kernels: 0 us -> 56.9 us
  waiting for transfers between devices: 56 us -> 0 us
  matrix products: 21.5 us -> 0 us
  between operations: 19.3 us -> 0.64 us
  starting transfers between devices: 5.73 us -> 0 us
  local copies, waits for them, and re-layouts: 11.5 us -> 6.67 us
  other arithmetic: 1.87 us -> 0 us
    pallas_call x0 -> x1, Pallas kernels: none -> 56.9 us  [on_device_fused(): pl.pallas_call(fused_kernel, out_shape=(pltpu.VMEM((depth, wide), f32), p...]
    ppermute x8 -> x0, waiting for transfers between devices: 47.1 us -> none  [from_behind(): lax.ppermute(array, axis, [(i, (i + by) % count) for i in range(count)])]
    dot_general x2 -> x0, matrix products: 21.5 us -> none  [the longest x1 11.3 us: on_device(): grad_here = jnp.dot(acts.T, whole_grad, preferred_element_type=jnp.float32)]
    all_gather x1 -> x0, waiting for transfers between devices: 8.25 us -> none  [on_device(): whole_grad = lax.all_gather(local_cols, 'tensor', axis=1, tiled=True)]
    ppermute x8 -> x0, starting transfers between devices: 5.69 us -> none  [from_behind(): lax.ppermute(array, axis, [(i, (i + by) % count) for i in range(count)])]
    slice x2 -> x0, local copies, waits for them, and re-layouts: 4.89 us -> none  [the longest x1 3.25 us: bucket_gossip(): source_array[:, :, bucket_index * bucket_width:(bucket_index + 1) * bucke...]
    convert_element_type x8 -> x0, other arithmetic: 1.87 us -> none  [fetch_peer(): part.astype(own.dtype)]
    unnamed x21 -> x4, local copies, waits for them, and re-layouts: 5.81 us -> 6.67 us
  transfers between devices with their start and end apart: 9 -> 0, of which waited for: 9 -> 0; matrix products, arithmetic and copies ran while one was open for 12% -> 0% of each run, Pallas kernels for 0% -> 0%
where the time goes in v1:
time: 64.4 us; the launch traced here: 64.3 us
  Pallas kernels  56.9 us (88%)
  local copies, waits for them, and re-layouts  6.67 us (10%)
    pallas_call x1, Pallas kernels, on_device_fused(): pl.pallas_call(fused_kernel, out_shape=(pltpu.VMEM((depth, wide), f32), p...  56.9 us
    unnamed x4, local copies, waits for them, and re-layouts  6.67 us

profile of v1, /device:TPU:0, one launch (start us, length us, event | category | flops | bytes accessed | tf_op | source)
XLA Modules:
  0.0 64.3 jit_solution(9313153822352517701)
XLA Ops:
  0.6 56.9 %shard_map.93 = (f32[1024,1024]{1,0:T(8,128)S(1)}, bf16[1024,1024]{1,0:T(8,128)(2,1)S(1)}, bf16[1024,1024]{1,0:T(8,128)(2,1)S(1)}, bf16[2048,1024]{1,0:T(8,128)(2,1)S(1)}) custom-call(s32[8]{0:T(128)} %exponent.1, bf16[2048,1024]{1,0:T(8,128)(2,1)} %bitcast.13, bf16[2048,128]{1,0:T(8,128)(2,1)} %bitcast.17, f32[1024,1024]{1,0:T(8,128)} %bitcast.14, ...), custom_call_target="tpu_custom_call" | custom-call | tf_op jit(solution)/shard_map/pallas_call | solution.py:321
  57.6 2.0 %copy.14 = f32[1,1024,1024]{2,1,0:T(8,128)} copy(f32[1,1024,1024]{2,1,0:T(8,128)S(1)} %bitcast.10) | data formatting | bytes 8388608
  59.6 1.3 %copy.15 = bf16[1,1024,1024]{2,1,0:T(8,128)(2,1)} copy(bf16[1,1024,1024]{2,1,0:T(8,128)(2,1)S(1)} %bitcast.12) | data formatting | bytes 4194304
  60.9 1.3 %copy.16 = bf16[1,1024,1024]{2,1,0:T(8,128)(2,1)} copy(bf16[1,1024,1024]{2,1,0:T(8,128)(2,1)S(1)} %bitcast.11) | data formatting | bytes 4194304
  62.2 2.0 %copy.17 = bf16[1,2048,1024]{2,1,0:T(8,128)(2,1)} copy(bf16[1,2048,1024]{2,1,0:T(8,128)(2,1)S(1)} %bitcast.9) | data formatting | bytes 8388608

commit v2 on v1

--- a/solution.py
+++ b/solution.py
@@ -79,11 +79,33 @@
 TILE = 256
 
 
+HALF = CHUNKS // 2
+
+
+def plane_order(z):
+    return [
+        z,
+        jnp.where(z == 0, 1, jnp.where(z == 1, 0, jnp.where(z == 2, 3, 2))),
+        jnp.where(z == 0, 2, jnp.where(z == 1, 2, 1)),
+        jnp.where(z < 2, 3, 0),
+    ]
+
+
+def adam_tile(averaged, grad, first_part, second_part):
+    first = beta_first * first_part.astype(jnp.float32) + (1.0 - beta_first) * grad
+    second = (
+        beta_second * second_part.astype(jnp.float32) + (1.0 - beta_second) * grad * grad
+    )
+    direction = first / (jnp.sqrt(second) + epsilon)
+    new_weights = averaged - learn_rate * (direction + decay_rate * averaged)
+    return (new_weights, first.astype(jnp.bfloat16), second.astype(jnp.bfloat16))
+
+
 def fused_kernel(
     exponent, tokens, kv_grad, weights, first_moment, second_moment,
-    new_weights, new_first, new_second, input_grad,
-    gathered, tok, tok_t, master, low, other, outgoing, incoming, first_in, second_in, grad_acc, back_acc,
-    up_sem, down_sem, across_sem, block_sem, core_send, core_recv, peer_send, peer_recv,
+    master, first_in, second_in, input_grad, grad_acc,
+    gathered, tok, tok_t, low, other, outgoing, incoming, back_acc,
+    up_sem, down_sem, across_sem, far_sem, block_sem, core_send, core_recv, peer_send, peer_recv,
     own_sem, master_sem, tok_sem, first_sem, second_sem,
 ):
     replica = lax.axis_index("replica")
@@ -103,12 +125,8 @@
     has_above = z < PLANES - 1
     has_below = z > 0
 
-    order = [
-        z,
-        jnp.where(z == 0, 1, z - 1),
-        jnp.where(z == 0, 2, jnp.where(z == 1, 2, jnp.where(z == 2, 3, 1))),
-        jnp.where(z < 2, 3, 0),
-    ]
+    order = plane_order(z)
+    at_end = jnp.logical_or(z == 0, z == PLANES - 1)
 
     def rows(c):
         return pl.ds(c * rows_of, rows_of)
@@ -124,6 +142,14 @@
             device_id=target, device_id_type=pl.DeviceIdType.MESH,
         )
 
+    def far_hop(plane, c, target, way):
+        block = plane * 2 + 1 - x
+        piece = gathered.at[block, rows(c)]
+        return pltpu.make_async_remote_copy(
+            src_ref=piece, dst_ref=piece, send_sem=far_sem.at[way, c], recv_sem=block_sem.at[block, c],
+            device_id=target, device_id_type=pl.DeviceIdType.MESH,
+        )
+
     def arrived(block, c):
         piece = gathered.at[block, rows(c)]
         pltpu.make_async_remote_copy(
@@ -137,9 +163,9 @@
             device_id=twin, device_id_type=pl.DeviceIdType.MESH,
         )
 
-    def to_peer(g):
+    def to_peer(i):
         return pltpu.make_async_remote_copy(
-            src_ref=outgoing.at[g], dst_ref=incoming.at[g], send_sem=peer_send.at[g], recv_sem=peer_recv.at[g],
+            src_ref=outgoing.at[i], dst_ref=incoming.at[i], send_sem=peer_send.at[i], recv_sem=peer_recv.at[i],
             device_id=peer, device_id_type=pl.DeviceIdType.MESH,
         )
 
@@ -186,27 +212,35 @@
 
         hop(z, c, across, across_sem).start()
 
-    for g in buckets:
+    near = [jnp.where(exponent[g] == 0, 1, 0) for g in buckets]
+    passed = []
+    for i in range(BLOCKS):
+        passed.append(near[i] if i == 0 else jnp.maximum(passed[-1], near[i]))
+
+    def mask(flag):
+        flags = jnp.full((16, width), flag, jnp.int32)
+        return jnp.where(flags == 1, 1.0, 0.0)[0:1]
+
+    def mix(flag, one, zero):
+        return one.astype(jnp.float32) * flag + zero.astype(jnp.float32) * (1.0 - flag)
+
+    for i, g in enumerate(buckets):
         load_master(g).wait()
         low[g] = master[:, columns(g)].astype(jnp.bfloat16)
         to_twin(g).start()
-
-        @pl.when(core == 1)
-        def _():
-            outgoing[g] = low[g]
-            to_peer(g).start()
-
-    for g in buckets:
+        if i > 0:
+            @pl.when(core == 1)
+            def _():
+                outgoing[i - 1] = mix(mask(passed[i - 1]), low[g], low[buckets[i - 1]]).astype(jnp.bfloat16)
+                to_peer(i - 1).start()
+
+    for i, g in enumerate(buckets):
         to_twin(g).wait_recv()
 
         @pl.when(core == 0)
         def _():
-            near = jnp.full((16, width), exponent[g], jnp.int32).astype(jnp.float32)
-            near = jnp.where(near == 0.0, 1.0, 0.0)[0:1]
-            outgoing[g] = (
-                other[g].astype(jnp.float32) * near + low[g].astype(jnp.float32) * (1.0 - near)
-            ).astype(jnp.bfloat16)
-            to_peer(g).start()
+            outgoing[i] = mix(mask(near[i]), other[g], low[g]).astype(jnp.bfloat16)
+            to_peer(i).start()
 
     for c in range(CHUNKS):
         load_tok[c].wait()
@@ -239,32 +273,38 @@
             else:
                 input_grad[part, tile] = (back_acc[part, tile] + term).astype(jnp.bfloat16)
 
-    def update(plane):
+    def update(phase):
         for side in range(2):
-            g = plane * 2 + side
-            to_peer(g).wait_recv()
-            near = jnp.full((16, width), exponent[g], jnp.int32).astype(jnp.float32)
-            near = jnp.where(near == 0.0, 1.0, 0.0)[0:1] * core.astype(jnp.float32)
+            i = (phase - 1) * 2 + side
+            g = buckets[i]
+            if i < BLOCKS - 1:
+                to_peer(i).wait_recv()
+            else:
+                @pl.when(core == 0)
+                def _():
+                    to_peer(i).wait_recv()
+
+            on_one = core
+            own_chip = mask(near[i] * on_one)
+            earlier = mask(passed[i] * on_one)
 
             @pl.loop(0, depth // TILE)
-            def _(i):
-                tile = pl.ds(pl.multiple_of(i * TILE, TILE), TILE)
+            def _(n):
+                tile = pl.ds(pl.multiple_of(n * TILE, TILE), TILE)
                 at = columns(g)
                 grad = grad_acc[tile, side * width:(side + 1) * width]
-                partner = (
-                    other[g, tile].astype(jnp.float32) * near
-                    + incoming[g, tile].astype(jnp.float32) * (1.0 - near)
-                )
-                averaged = 0.5 * (master[tile, at] + partner)
-                first = beta_first * first_in[tile, at].astype(jnp.float32) + (1.0 - beta_first) * grad
-                second = (
-                    beta_second * second_in[tile, at].astype(jnp.float32)
-                    + (1.0 - beta_second) * grad * grad
-                )
-                direction = first / (jnp.sqrt(second) + epsilon)
-                new_weights[tile, at] = averaged - learn_rate * (direction + decay_rate * averaged)
-                new_first[tile, at] = first.astype(jnp.bfloat16)
-                new_second[tile, at] = second.astype(jnp.bfloat16)
+                here = incoming[i, tile].astype(jnp.float32)
+                if i == BLOCKS - 1:
+                    here = jnp.where(mask(on_one) == 1.0, incoming[i - 1, tile].astype(jnp.float32), here)
+                elif i > 0:
+                    here = mix(earlier, incoming[i - 1, tile], here)
+                averaged = 0.5 * (master[tile, at] + mix(own_chip, other[g, tile], here))
+                if phase == PLANES:
+                    master[tile, at] = averaged
+                else:
+                    master[tile, at], first_in[tile, at], second_in[tile, at] = adam_tile(
+                        averaged, grad, first_in[tile, at], second_in[tile, at]
+                    )
 
     for phase in range(1, PLANES + 1):
         for c in range(CHUNKS):
@@ -287,18 +327,56 @@
                     def _():
                         hop(plane, c, below, down_sem).start()
 
-                hop(order[phase], c, across, across_sem).start()
+                if c < HALF or phase == 2:
+                    hop(order[phase], c, across, across_sem).start()
+                elif phase == 1:
+                    @pl.when(at_end)
+                    def _():
+                        hop(order[phase], c, across, across_sem).start()
             plane = order[phase - 1]
-            arrived(plane * 2 + 1 - x, c)
+            away = plane * 2 + 1 - x
+            if c < HALF or phase < PLANES:
+                arrived(away, c)
+            else:
+                @pl.when(at_end)
+                def _():
+                    arrived(away, c)
+            if c >= HALF and phase < 3:
+                turn = (0, PLANES - 1) if phase == 1 else (1, PLANES - 2)
+
+                @pl.when(z == turn[0])
+                def _():
+                    far_hop(plane, c, above, 0).start()
+
+                @pl.when(z == turn[1])
+                def _():
+                    far_hop(plane, c, below, 1).start()
+            if c >= HALF and phase == 3:
+                @pl.when(jnp.logical_not(at_end))
+                def _():
+                    arrived(order[3] * 2 + 1 - x, c)
+
+                @pl.when(z == 1)
+                def _():
+                    far_hop(order[3], c, below, 1).start()
+
+                @pl.when(z == 2)
+                def _():
+                    far_hop(order[3], c, above, 0).start()
             multiply(plane, c, "first" if phase == 1 else "middle" if phase < PLANES else "last")
         if phase == 1:
             load_first.wait()
             load_second.wait()
-        update(plane)
+        update(phase)
 
     for c in range(CHUNKS):
         for plane in range(PLANES):
-            hop(plane, c, across, across_sem).wait_send()
+            if c < HALF or plane in (0, 2):
+                hop(order[plane], c, across, across_sem).wait_send()
+            elif plane == 1:
+                @pl.when(at_end)
+                def _():
+                    hop(order[plane], c, across, across_sem).wait_send()
 
             @pl.when(jnp.logical_and(has_above, plane <= z))
             def _():
@@ -308,9 +386,67 @@
             def _():
                 hop(plane, c, below, down_sem).wait_send()
 
+        if c >= HALF:
+            @pl.when(has_above)
+            def _():
+                far_hop(0, c, above, 0).wait_send()
+
+            @pl.when(has_below)
+            def _():
+                far_hop(PLANES - 1, c, below, 1).wait_send()
+
     for g in range(BLOCKS):
         to_twin(g).wait_send()
-        to_peer(g).wait_send()
+    for i in range(BLOCKS - 1):
+        to_peer(i).wait_send()
+
+    @pl.when(core == 0)
+    def _():
+        to_peer(BLOCKS - 1).wait_send()
+
+
+def finish_kernel(
+    averaged, first_in, second_in, back, grad_acc, new_weights, new_first, new_second, input_grad,
+    weights_out, first_out, second_out, pair_sem, back_sem, last_sem,
+):
+    order = plane_order(lax.div(lax.axis_index("tensor"), 2))
+    depth, wide = grad_acc.shape
+    rows_of = back.shape[0] // CHUNKS
+    half = depth // 2
+
+    def columns(plane):
+        return pl.ds(pl.multiple_of(plane * wide, wide), wide)
+
+    copies = []
+    for i in range(PLANES - 1):
+        at = columns(order[i])
+        for k, (source, target) in enumerate(
+            ((averaged, new_weights), (first_in, new_first), (second_in, new_second))
+        ):
+            copies.append(pltpu.make_async_copy(source.at[:, at], target.at[:, at], pair_sem.at[i, k]))
+    for c in range(CHUNKS):
+        part = pl.ds(c * rows_of, rows_of)
+        copies.append(pltpu.make_async_copy(back.at[part], input_grad.at[part], back_sem.at[c]))
+    for copy in copies:
+        copy.start()
+    at = columns(order[PLANES - 1])
+    for h in range(2):
+        @pl.loop(0, half // 128)
+        def _(n):
+            tile = pl.ds(pl.multiple_of(h * half + n * 128, 128), 128)
+            weights_out[tile], first_out[tile], second_out[tile] = adam_tile(
+                averaged[tile, at], grad_acc[tile], first_in[tile, at], second_in[tile, at]
+            )
+
+        part = pl.ds(h * half, half)
+        for k, (source, target) in enumerate(
+            ((weights_out, new_weights), (first_out, new_first), (second_out, new_second))
+        ):
+            copy = pltpu.make_async_copy(source.at[part], target.at[part, at], last_sem.at[h, k])
+            copy.start()
+            copies.append(copy)
+    for copy in copies:
+        copy.wait()
 
 
 def on_device_fused(tokens, kv_grad, weights, first_moment, second_moment, exponent):
@@ -325,25 +461,23 @@
             pltpu.VMEM((depth, wide), bf16),
             pltpu.VMEM((depth, wide), bf16),
             pltpu.VMEM((tok, depth), bf16),
+            pltpu.VMEM((depth, 2 * width), f32),
         ),
         in_specs=[pl.BlockSpec(memory_space=pltpu.SMEM)] + [any_space] * 5,
-        out_specs=[pl.BlockSpec(memory_space=pltpu.VMEM)] * 4,
+        out_specs=[pl.BlockSpec(memory_space=pltpu.VMEM)] * 5,
         scratch_shapes=[
             pltpu.VMEM((BLOCKS, tok, width), bf16),
             pltpu.VMEM((tok, depth), bf16),
             pltpu.VMEM((depth, tok), bf16),
-            pltpu.VMEM((depth, wide), f32),
             pltpu.VMEM((BLOCKS, depth, width), bf16),
             pltpu.VMEM((BLOCKS, depth, width), bf16),
             pltpu.VMEM((BLOCKS, depth, width), bf16),
             pltpu.VMEM((BLOCKS, depth, width), bf16),
-            pltpu.VMEM((depth, wide), bf16),
-            pltpu.VMEM((depth, wide), bf16),
-            pltpu.VMEM((depth, 2 * width), f32),
             pltpu.VMEM((tok, depth), f32),
             pltpu.SemaphoreType.DMA((PLANES, CHUNKS)),
             pltpu.SemaphoreType.DMA((PLANES, CHUNKS)),
             pltpu.SemaphoreType.DMA((PLANES, CHUNKS)),
+            pltpu.SemaphoreType.DMA((2, CHUNKS)),
             pltpu.SemaphoreType.DMA((BLOCKS, CHUNKS)),
             pltpu.SemaphoreType.DMA((BLOCKS,)),
             pltpu.SemaphoreType.DMA((BLOCKS,)),
@@ -359,7 +493,27 @@
             collective_id=0, has_side_effects=True, vmem_limit_bytes=46 << 20
         ),
     )(exponent, tokens[0], kv_grad[0], weights[0], first_moment[0], second_moment[0])
-    return tuple(out[None] for out in outs)
+    results = pl.pallas_call(
+        finish_kernel,
+        out_shape=(
+            jax.ShapeDtypeStruct((depth, wide), f32),
+            jax.ShapeDtypeStruct((depth, wide), bf16),
+            jax.ShapeDtypeStruct((depth, wide), bf16),
+            jax.ShapeDtypeStruct((tok, depth), bf16),
+        ),
+        in_specs=[pl.BlockSpec(memory_space=pltpu.VMEM)] * 5,
+        out_specs=[any_space] * 4,
+        scratch_shapes=[
+            pltpu.VMEM((depth, 2 * width), f32),
+            pltpu.VMEM((depth, 2 * width), bf16),
+            pltpu.VMEM((depth, 2 * width), bf16),
+            pltpu.SemaphoreType.DMA((PLANES - 1, 3)),
+            pltpu.SemaphoreType.DMA((CHUNKS,)),
+            pltpu.SemaphoreType.DMA((2, 3)),
+        ],
+        compiler_params=pltpu.CompilerParams(vmem_limit_bytes=24 << 20),
+    )(*outs)
+    return tuple(out[None] for out in results)
 
 
 def solution(mesh):

time: 64.4 us -> 60.7 us (0.943)
  local copies, waits for them, and re-layouts: 6.67 us -> 0 us
  Pallas kernels: 56.9 us -> 59.9 us
    unnamed x4 -> x0, local copies, waits for them, and re-layouts: 6.67 us -> none
    pallas_call x0 -> x1, Pallas kernels: none -> 4.7 us  [on_device_fused(): pl.pallas_call(finish_kernel, out_shape=(jax.ShapeDtypeStruct((depth, wid...]
    pallas_call x1, Pallas kernels: 56.9 us -> 55.2 us  [on_device_fused(): pl.pallas_call(fused_kernel, out_shape=(pltpu.VMEM((depth, wide), f32), p...]
where the time goes in v2:
time: 60.7 us; the launch traced here: 60.5 us
  Pallas kernels  59.9 us (99%)
  between operations  0.64 us (1%)
    pallas_call x1, Pallas kernels, on_device_fused(): pl.pallas_call(fused_kernel, out_shape=(pltpu.VMEM((depth, wide), f32), p...  55.2 us
    pallas_call x1, Pallas kernels, on_device_fused(): pl.pallas_call(finish_kernel, out_shape=(jax.ShapeDtypeStruct((depth, wid...  4.7 us

profile of v2, /device:TPU:0, one launch (start us, length us, event | category | flops | bytes accessed | tf_op | source)
XLA Modules:
  0.0 60.5 jit_solution(8407026857191775393)
XLA Ops:
  0.6 55.2 %shard_map.93 = (f32[1024,1024]{1,0:T(8,128)S(1)}, bf16[1024,1024]{1,0:T(8,128)(2,1)S(1)}, bf16[1024,1024]{1,0:T(8,128)(2,1)S(1)}, bf16[2048,1024]{1,0:T(8,128)(2,1)S(1)}, f32[1024,256]{1,0:T(8,128)S(1)}) custom-call(s32[8]{0:T(128)} %exponent.1, bf16[2048,1024]{1,0:T(8,128)(2,1)} %bitcast.9, bf16[2048,128]{1,0:T(8,128)(2,1)} %bitcast.13, ...), custom_call_target="tpu_custom_call" | custom-call | tf_op jit(solution)/shard_map/pallas_call | solution.py:457
  55.8 4.7 %shard_map.94 = (f32[1024,1024]{1,0:T(8,128)}, bf16[1024,1024]{1,0:T(8,128)(2,1)}, bf16[1024,1024]{1,0:T(8,128)(2,1)}, bf16[2048,1024]{1,0:T(8,128)(2,1)}) custom-call(f32[1024,1024]{1,0:T(8,128)S(1)} %get-tuple-element.13.averaged, bf16[1024,1024]{1,0:T(8,128)(2,1)S(1)} %get-tuple-element.14.first_in, bf16[1024,1024]{1,0:T(8,128)(2,1)S(1)} %get-tuple-element.15.second_in, ...), custom_call_target="tpu_custom_call" | custom-call | tf_op jit(solution)/shard_map/pallas_call | solution.py:496

commit v3 on v2

--- a/solution.py
+++ b/solution.py
@@ -179,12 +179,8 @@
     for g in buckets:
         load_master(g).start()
     load_tok = [pltpu.make_async_copy(tokens.at[rows(c)], tok.at[rows(c)], tok_sem.at[c]) for c in range(CHUNKS)]
-    for copy in load_tok:
-        copy.start()
     load_first = pltpu.make_async_copy(first_moment, first_in, first_sem)
     load_second = pltpu.make_async_copy(second_moment, second_in, second_sem)
-    load_first.start()
-    load_second.start()
 
     barrier = pltpu.get_barrier_semaphore()
     for target in (across, twin, peer):
@@ -233,6 +229,11 @@
             def _():
                 outgoing[i - 1] = mix(mask(passed[i - 1]), low[g], low[buckets[i - 1]]).astype(jnp.bfloat16)
                 to_peer(i - 1).start()
+
+    for copy in load_tok:
+        copy.start()
+    load_first.start()
+    load_second.start()
 
     for i, g in enumerate(buckets):
         to_twin(g).wait_recv()
@@ -307,7 +308,7 @@
                     )
 
     for phase in range(1, PLANES + 1):
-        for c in range(CHUNKS):
+        for c in range(CHUNKS) if phase < PLANES else (0, 2, 1, 3):
             if phase < PLANES:
                 @pl.when(z - phase >= 0)
                 def _():

time: 60.7 us -> 59.8 us (0.985)
  Pallas kernels: 59.9 us -> 59 us
    pallas_call x1, Pallas kernels: 55.2 us -> 54.3 us  [on_device_fused(): pl.pallas_call(fused_kernel, out_shape=(pltpu.VMEM((depth, wide), f32), p...]
where the time goes in v3:
time: 59.8 us; the launch traced here: 59.6 us
  Pallas kernels  59 us (99%)
  between operations  0.64 us (1%)
    pallas_call x1, Pallas kernels, on_device_fused(): pl.pallas_call(fused_kernel, out_shape=(pltpu.VMEM((depth, wide), f32), p...  54.3 us
    pallas_call x1, Pallas kernels, on_device_fused(): pl.pallas_call(finish_kernel, out_shape=(jax.ShapeDtypeStruct((depth, wid...  4.7 us

profile of v3, /device:TPU:0, one launch (start us, length us, event | category | flops | bytes accessed | tf_op | source)
XLA Modules:
  0.0 59.6 jit_solution(7965459982707668626)
XLA Ops:
  0.6 54.3 %shard_map.93 = (f32[1024,1024]{1,0:T(8,128)S(1)}, bf16[1024,1024]{1,0:T(8,128)(2,1)S(1)}, bf16[1024,1024]{1,0:T(8,128)(2,1)S(1)}, bf16[2048,1024]{1,0:T(8,128)(2,1)S(1)}, f32[1024,256]{1,0:T(8,128)S(1)}) custom-call(s32[8]{0:T(128)} %exponent.1, bf16[2048,1024]{1,0:T(8,128)(2,1)} %bitcast.9, bf16[2048,128]{1,0:T(8,128)(2,1)} %bitcast.13, ...), custom_call_target="tpu_custom_call" | custom-call | tf_op jit(solution)/shard_map/pallas_call | solution.py:458
  54.9 4.7 %shard_map.94 = (f32[1024,1024]{1,0:T(8,128)}, bf16[1024,1024]{1,0:T(8,128)(2,1)}, bf16[1024,1024]{1,0:T(8,128)(2,1)}, bf16[2048,1024]{1,0:T(8,128)(2,1)}) custom-call(f32[1024,1024]{1,0:T(8,128)S(1)} %get-tuple-element.13.averaged, bf16[1024,1024]{1,0:T(8,128)(2,1)S(1)} %get-tuple-element.14.first_in, bf16[1024,1024]{1,0:T(8,128)(2,1)S(1)} %get-tuple-element.15.second_in, ...), custom_call_target="tpu_custom_call" | custom-call | tf_op jit(solution)/shard_map/pallas_call | solution.py:497
